TPU v7x, 256 devices: a whole 4x4x8 slice. The times are simulated.
256 devices in a mesh: gx: 16 (over z_lo, y, core), gy: 16 (over x, z_hi).
Axes of the slice: x: 4, y: 4, z: 8 (z_hi: 4, z_lo: 2; z = z_hi * 2 + z_lo), core: 2. Of those that a mesh axis runs over, the one named last changes fastest.
Arguments:
- field: float32 [1, 20, 128, 128, 768], P(None, None, 'gx', 'gy'), may hold values from -6 to 6
- spec_weight: float32 [20, 20, 24, 9216], P(None, None, None, ('gx', 'gy')), may hold values from -2.5 to 2.5
- bypass_weight: float32 [20, 20], replicated, may hold values from -1.25 to 1.25
- bypass_bias: float32 [20], replicated, may hold values from -3 to 3
Outputs:
- activated: float32 [1, 20, 128, 128, 768], P(None, None, 'gx', 'gy')
All inputs are finite; a program needn't handle non-finite values.
Results may differ from a plain program's by a relative error of at most 0.00005.
Values sent between devices are 32-bit elements; how exact they have to be, the bound alone decides.
No kernel may reach another device: no remote copies, remote signals or barrier semaphores. Data moves between devices by JAX's collectives and lax.ppermute only.
A program may use at most 128 MiB of HBM per device.

v0:
```python
import math

import jax
import jax.numpy as jnp
import ml_dtypes
import numpy as np
from jax import lax
from jax.experimental import pallas as pl
from jax.experimental.pallas import tpu as pltpu
from jax.sharding import PartitionSpec as P

C, NX, NY, NZ, NT = 20, 128, 128, 32, 24
KX, KY, KZ, KT = 24, 24, 16, 12
ZT, MZT = NZ * NT, KZ * KT
GX = GY = 16
RX, RY = NX // GX, NY // GY
BM = MZT // GX
H = BM * KX // GY
HQ = 2 * H
CM, CR = 16, 4
MAIN = BM * 2 * RX
ROWS = MAIN + BM * 2 * RX * CR // CM
HALF = ZT // 2
LANES = 768
MIB = 1024 * 1024

NN = (((1,), (0,)), ((), ()))
NT_DIMS = (((1,), (1,)), ((), ()))


GY_ORDER = [x * 4 + z for z in range(4) for x in range(4)]


def slot_mode(slot):
    return (slot % 4) * 3 + slot // 4


def kept(count, length):
    steps = np.arange(count)
    return np.where(steps < count // 2, steps, length - count + steps)


def halves(table):
    table = table.astype(np.float32)
    high = table.astype(ml_dtypes.bfloat16)
    low = (table - high.astype(np.float32)).astype(ml_dtypes.bfloat16)
    return np.stack([high, low])


def depth_table():
    kz = kept(KZ, NZ)
    modes = np.array([g * BM + slot_mode(s) for g in range(GX) for s in range(BM)])
    z_freq, t_freq = kz[modes // KT], modes % KT
    cells = np.arange(ZT)
    turns = (z_freq[:, None] * (cells // NT)[None] * NT + t_freq[:, None] * (cells % NT)[None] * NZ) % ZT
    angle = turns * (2.0 * np.pi / ZT)
    cosine, sine = np.cos(angle), np.sin(angle)
    scale = (np.where(t_freq == 0, 1.0, 2.0) / (NX * NY * ZT))[:, None]
    inverse = np.stack([cosine * scale, -sine * scale], axis=1).reshape(2 * MZT, ZT)
    return right_table(inverse)


def x_tables():
    angle = (np.arange(NX)[:, None] * kept(KX, NX)[None] % NX) * (2.0 * np.pi / NX)
    cosine, sine = np.cos(angle), np.sin(angle)
    forward = np.stack([np.stack([cosine, -sine], -1), np.stack([sine, cosine], -1)], 1)
    back = np.stack([np.stack([cosine, -sine], -1), np.stack([sine, cosine], -1)], 1)
    shape = (GX, RX, 2, KX * 2)
    forward, back = forward.reshape(shape), back.reshape(shape)
    def main(table):
        return table.transpose(0, 2, 1, 3).reshape(GX * 2 * RX, KX * 2)
    def rest(table):
        return table.reshape(GX * RX * 2, KX * 2)
    return (
        np.stack([left_table(main(forward).T), left_table(rest(forward).T)]),
        np.stack([left_table(main(back)), left_table(rest(back))]),
    )


def y_tables():
    angle = (np.arange(NY)[:, None] * kept(KY, NY)[None] % NY) * (2.0 * np.pi / NY)
    cosine, sine = np.cos(angle), np.sin(angle)
    both = np.concatenate([cosine, sine], axis=1)
    both = both.reshape(GY, RY, 2 * KY)[np.array(GY_ORDER)].reshape(NY, 2 * KY)
    return left_table(both.T), left_table(both)


def split(value):
    high = value.astype(jnp.bfloat16)
    return high, (value - high.astype(jnp.float32)).astype(jnp.bfloat16)


def stacked_left(value, axis):
    high, low = split(value)
    return jnp.concatenate([high, high, low], axis=axis)


def stacked_right(value, axis):
    high, low = split(value)
    return jnp.concatenate([high, low, high], axis=axis)


def left_table(table):
    high, low = halves(table)
    return np.concatenate([high, high, low], axis=1)


def right_table(table):
    high, low = halves(table)
    return np.concatenate([high, low, high], axis=0)


def dot(left, right, dims):
    return lax.dot_general(left, right, dims, preferred_element_type=jnp.float32)


def block_swap(value):
    row = lax.broadcasted_iota(jnp.int32, value.shape, 1) // 2
    lane = lax.broadcasted_iota(jnp.int32, value.shape, 2) // 32
    far = pltpu.roll(pltpu.roll(value, 4, 1), 64, 2)
    value = jnp.where((row // 2) == (lane // 2), value, far)
    up = pltpu.roll(pltpu.roll(value, 6, 1), 32, 2)
    down = pltpu.roll(pltpu.roll(value, 2, 1), 96, 2)
    return jnp.where((row % 2) == (lane % 2), value, jnp.where(row % 2 == 0, up, down))


def divide(value, by):
    return (value * 2731) >> 16 if by == 24 else value // by


def cos_sin(index, length):
    half = (index - length // 2).astype(jnp.float32) * np.float32(np.pi / length)
    square = half * half
    sine, cosine = jnp.zeros_like(half), jnp.zeros_like(half)
    for power in range(14, -1, -2):
        sign = -1.0 if power % 4 else 1.0
        cosine = cosine * square + np.float32(sign / math.factorial(power))
        sine = sine * square + np.float32(sign / math.factorial(power + 1))
    sine = sine * half
    return 2.0 * sine * sine - 1.0, -2.0 * sine * cosine


def fill_forward_table(table):
    def cells(rows):
        row = lax.broadcasted_iota(jnp.int32, (rows, HALF), 0)
        lane = lax.broadcasted_iota(jnp.int32, (rows, HALF), 1)
        z = divide(lane, NT)
        return row, z, lane - NT * z
    row, z, _ = cells(GX)
    z_freq = jnp.where(row < KZ // 2, row, row + NZ - KZ)
    z_cos, z_sin = cos_sin((z_freq * z) % NZ, NZ)
    row, _, t = cells(2 * BM)
    slot = row >> 1
    turns = ((slot & 3) * 3 + (slot >> 2)) * t
    t_cos, t_sin = cos_sin(turns - NT * divide(turns, NT), NT)
    real = (row & 1) == 0
    one = jnp.where(real, t_cos, -t_sin)
    two = jnp.where(real, -t_sin, -t_cos)
    for odd in range(2):
        rows = [z_cos[g : g + 1] * one + z_sin[g : g + 1] * two for g in range(odd, GX, 2)]
        table[odd] = jnp.concatenate(split(jnp.concatenate(rows, axis=0)), axis=0)


def depth_modes(cells, table):
    near, far = cells[:, :HALF], cells[:, HALF:]
    modes = []
    for odd in range(2):
        high, low = split(near - far if odd else near + far)
        both = dot(table[odd], high, NT_DIMS)
        modes.append(both[:MZT] + (both[MZT:] + dot(table[odd, :MZT], low, NT_DIMS)))
    return modes


def depth_kernel(field, out, held, table, arrived):
    copies = [
        pltpu.make_async_copy(field.at[:, pl.ds(2 * pair, 2)], held.at[pair], arrived.at[pair])
        for pair in range(4)
    ]
    for copy in copies:
        copy.start()
    fill_forward_table(table)
    for pair in range(4):
        if pair < 2:
            for copy in copies[pair : 1 + 3 * pair]:
                copy.wait()
        cells = jnp.concatenate(
            [held[pair, 0:CM, k].reshape(CM * RY, ZT) for k in range(2)], axis=0
        )
        modes = depth_modes(cells, table)
        for k in range(2):
            for dest in range(GX):
                start = dest * ROWS + 2 * pair + k
                row = dest // 2 * 2 * BM
                out[pl.ds(start, 2 * BM, stride=RX), :] = modes[dest % 2][
                    row : row + 2 * BM, k * 128 : (k + 1) * 128
                ]
    cells = jnp.concatenate(
        [held[k // 2, CM:C, k % 2].reshape(CR * RY, ZT) for k in range(RX)], axis=0
    )
    modes = depth_modes(cells, table)
    for half in range(2):
        for odd in range(2):
            tiles = block_swap(modes[odd][:, half * 128 : (half + 1) * 128].reshape(GX // 2 * 3, 8, 128))
            for dest in range(odd, GX, 2):
                for third in range(3):
                    start = dest * ROWS + MAIN + third * 16 + half * 8
                    out[pl.ds(start, 8), :] = tiles[dest // 2 * 3 + third]


def depth_transform(field):
    return pl.pallas_call(
        depth_kernel,
        in_specs=[pl.BlockSpec(memory_space=pltpu.HBM)],
        out_shape=jax.ShapeDtypeStruct((GX * ROWS, 128), jnp.float32),
        scratch_shapes=[
            pltpu.VMEM((4, C, 2, RY, ZT), jnp.float32),
            pltpu.VMEM((2, 2 * MZT, HALF), jnp.bfloat16),
            pltpu.SemaphoreType.DMA((4,)),
        ],
        compiler_params=pltpu.CompilerParams(vmem_limit_bytes=50 * MIB),
        cost_estimate=pl.CostEstimate(flops=1200000000, bytes_accessed=6000000, transcendentals=0),
        name="depth_forward",
    )(field)


def x_kernel(cells, table, out):
    def modes_of(first, which):
        columns = jnp.concatenate(
            [cells[pl.ds(s * ROWS + first, 16), :] for s in range(GX)], axis=0
        )
        return dot(table[which], stacked_right(columns, 0), NN)

    slots = [0] * BM
    for slot in range(BM):
        slots[slot_mode(slot)] = slot
    for a in range(4):
        modes = jnp.concatenate([modes_of(slots[3 * a + m] * 16, 0) for m in range(3)], axis=0)
        for b in range(4):
            place = GY_ORDER.index(4 * a + b)
            turned = modes[b * HQ : (b + 1) * HQ].T
            for c in range(CM):
                out[place, :, c * HQ : (c + 1) * HQ] = turned[c * RY : (c + 1) * RY]
    modes = jnp.concatenate([modes_of(MAIN + m * 16, 1) for m in range(3)], axis=0)
    for b in range(4):
        turned = modes[b * HQ : (b + 1) * HQ].T
        for a in range(4):
            place = GY_ORDER.index(4 * a + b)
            for c in range(CR):
                row = (a * CR + c) * RY
                out[place, :, (CM + c) * HQ : (CM + c + 1) * HQ] = turned[row : row + RY]
            out[place, :, C * HQ : LANES] = jnp.zeros((RY, LANES - C * HQ), jnp.float32)


def x_transform(cells, table):
    return pl.pallas_call(
        x_kernel,
        out_shape=jax.ShapeDtypeStruct((GY, RY, LANES), jnp.float32),
        compiler_params=pltpu.CompilerParams(vmem_limit_bytes=40 * MIB),
        cost_estimate=pl.CostEstimate(flops=150000000, bytes_accessed=2500000, transcendentals=0),
        name="x_forward",
    )(cells, table)


def even_lanes(shape):
    return lax.broadcasted_iota(jnp.int32, shape, len(shape) - 1) % 2 == 0


def turn_parts(value, even):
    lanes = value.shape[-1]
    return jnp.where(even, -pltpu.roll(value, lanes - 1, 1), pltpu.roll(value, 1, 1))


def mix_kernel(cells, weights, forward, back, out, reals, imags, mixed):
    sums = dot(forward[...], stacked_right(cells[...].reshape(GY * RY, LANES), 0), NN)
    even = even_lanes((KY, LANES))
    coef = sums[:KY] - turn_parts(sums[KY:], even)
    real = jnp.where(even, coef, pltpu.roll(coef, 1, 1))
    imag = jnp.where(even, pltpu.roll(coef, LANES - 1, 1), coef)
    for i in range(C):
        reals[i] = real[:, i * HQ : (i + 1) * HQ]
        imags[i] = imag[:, i * HQ : (i + 1) * HQ]
    even_pairs = even_lanes((KY, HQ))
    group = 4
    for first in range(0, C, group):
        one = [jnp.zeros((KY, HQ), jnp.float32)] * group
        two = [jnp.zeros((KY, HQ), jnp.float32)] * group
        for i in range(C):
            real_i, imag_i = reals[i], imags[i]
            for k in range(group):
                weight = weights[i, first + k]
                one[k] = one[k] + weight * real_i
                two[k] = two[k] + weight * imag_i
        for k in range(group):
            o = first + k
            mixed[:, o * HQ : (o + 1) * HQ] = one[k] + turn_parts(two[k], even_pairs)
    mixed[:, C * HQ : LANES] = jnp.zeros((KY, LANES - C * HQ), jnp.float32)
    modes = mixed[...]
    both = jnp.concatenate([modes, turn_parts(modes, even)], axis=0)
    out[...] = dot(back[...], stacked_right(both, 0), NN).reshape(GY, RY, LANES)


def mix_modes(cells, weights, forward, back):
    return pl.pallas_call(
        mix_kernel,
        out_shape=jax.ShapeDtypeStruct((GY, RY, LANES), jnp.float32),
        scratch_shapes=[
            pltpu.VMEM((C, KY, HQ), jnp.float32),
            pltpu.VMEM((C, KY, HQ), jnp.float32),
            pltpu.VMEM((KY, LANES), jnp.float32),
        ],
        compiler_params=pltpu.CompilerParams(vmem_limit_bytes=40 * MIB),
        cost_estimate=pl.CostEstimate(flops=60000000, bytes_accessed=6000000, transcendentals=0),
        name="y_mix",
    )(cells, weights, forward, back)


def x_back_kernel(modes, table, out):
    def write(first, which, columns):
        cells = dot(table[which], stacked_right(columns, 0), NN)
        for s in range(GX):
            out[pl.ds(s * ROWS + first, 16), :] = cells[s * 16 : (s + 1) * 16]

    def columns_of(pieces):
        rows = jnp.concatenate(
            [modes[GY_ORDER.index(g), :, c * HQ : (c + 1) * HQ] for g, c in pieces], axis=0
        )
        return rows.T

    slots = [0] * BM
    for slot in range(BM):
        slots[slot_mode(slot)] = slot
    for a in range(4):
        parts = [columns_of([(4 * a + b, c) for c in range(CM)]) for b in range(4)]
        columns = jnp.concatenate(parts, axis=0)
        for m in range(3):
            write(slots[3 * a + m] * 16, 0, columns[m * 2 * KX : (m + 1) * 2 * KX])
    parts = [
        columns_of([(4 * a + b, CM + c) for a in range(4) for c in range(CR)]) for b in range(4)
    ]
    columns = jnp.concatenate(parts, axis=0)
    for m in range(3):
        write(MAIN + m * 16, 1, columns[m * 2 * KX : (m + 1) * 2 * KX])


def x_back(modes, table):
    return pl.pallas_call(
        x_back_kernel,
        out_shape=jax.ShapeDtypeStruct((GX * ROWS, 128), jnp.float32),
        compiler_params=pltpu.CompilerParams(vmem_limit_bytes=40 * MIB),
        cost_estimate=pl.CostEstimate(flops=150000000, bytes_accessed=2500000, transcendentals=0),
        name="x_back",
    )(modes, table)


def spread_map(channel_map):
    rows = C * RY
    copy = lax.broadcasted_iota(jnp.int32, (C, rows), 1) // RY
    copy = (copy == lax.broadcasted_iota(jnp.int32, (C, rows), 0)).astype(jnp.bfloat16)
    same = lax.broadcasted_iota(jnp.int32, (rows, rows), 0) % RY
    same = same == lax.broadcasted_iota(jnp.int32, (rows, rows), 1) % RY
    spread = []
    for half in split(channel_map):
        wide = lax.dot_general(half, copy, NN, preferred_element_type=jnp.float32)
        tall = jnp.broadcast_to(wide[:, None], (C, RY, rows)).reshape(rows, rows)
        spread.append(jnp.where(same, tall, 0.0).astype(jnp.bfloat16))
    return spread


def final_kernel(field, cells, table, channel_map, bias, out, held, left):
    high, low = spread_map(channel_map[...])
    spread = jnp.concatenate([high, high, low], axis=1)
    copies = []
    for pair in range(RX // 2):
        if pair % 2 == 0:
            tiles = jnp.stack(
                [
                    cells[pl.ds(s * ROWS + MAIN + third * 16 + (pair // 2) * 8, 8), :]
                    for s in range(GX)
                    for third in range(3)
                ]
            )
            rest = block_swap(tiles).reshape(2 * MZT, 128).T
        columns = []
        for k in range(2):
            main = jnp.concatenate(
                [cells[pl.ds(s * ROWS + 2 * pair + k, 2 * BM, stride=RX), :] for s in range(GX)],
                axis=0,
            )
            row = ((pair % 2) * 2 + k) * CR * RY
            columns += [main.T, rest[row : row + CR * RY]]
        spectral = dot(stacked_left(jnp.concatenate(columns, axis=0), 1), table[...], NN)
        for k in range(2):
            x = 2 * pair + k
            bypass = dot(spread, stacked_right(field[:, x].reshape(C * RY, ZT), 0), NN)
            value = spectral[k * C * RY : (k + 1) * C * RY] + bypass
            for c in range(C):
                one = value[c * RY : (c + 1) * RY] + bias[c]
                held[c, x] = 0.5 * one * (1.0 + lax.erf(one * np.float32(np.sqrt(0.5))))
                first = C // 2 if x == RX - 1 and c >= C // 2 else 0
                if c == C - 1 or (x == RX - 1 and c == C // 2 - 1):
                    part = pl.ds(first, c + 1 - first)
                    copy = pltpu.make_async_copy(
                        held.at[part, x], out.at[part, x], left.at[len(copies)]
                    )
                    copies.append(copy)
                    copy.start()
    for copy in copies:
        copy.wait()


def final_stage(field, cells, table, channel_map, bias):
    whole = pl.BlockSpec(memory_space=pltpu.VMEM)
    return pl.pallas_call(
        final_kernel,
        in_specs=[whole, whole, whole, whole, pl.BlockSpec(memory_space=pltpu.SMEM)],
        out_specs=pl.BlockSpec(memory_space=pltpu.HBM),
        out_shape=jax.ShapeDtypeStruct((C, RX, RY, ZT), jnp.float32),
        scratch_shapes=[
            pltpu.VMEM((C, RX, RY, ZT), jnp.float32),
            pltpu.SemaphoreType.DMA((RX + 1,)),
        ],
        compiler_params=pltpu.CompilerParams(vmem_limit_bytes=40 * MIB),
        cost_estimate=pl.CostEstimate(flops=3200000000, bytes_accessed=11000000, transcendentals=1000000),
        name="depth_back",
    )(field, cells, table, channel_map, bias)


def exchange(value, axis, groups=None):
    return lax.all_to_all(
        value, axis, split_axis=0, concat_axis=0, axis_index_groups=groups, tiled=True
    )


def shards(field, spec_weight, bypass_weight, bypass_bias):
    x_forward, x_inverse = x_tables()
    y_forward, y_inverse = y_tables()
    field = field.reshape(C, RX, RY, ZT)
    modes = depth_transform(field)
    cells = exchange(modes.reshape(GX, ROWS, 128), "gx").reshape(GX * ROWS, 128)
    pairs = exchange(x_transform(cells, x_forward), "gy", [GY_ORDER])
    mixed = exchange(mix_modes(pairs, spec_weight, y_forward, y_inverse), "gy", [GY_ORDER])
    back = x_back(mixed, x_inverse)
    back = exchange(back.reshape(GX, ROWS, 128), "gx").reshape(GX * ROWS, 128)
    out = final_stage(field, back, depth_table(), bypass_weight, bypass_bias)
    return out.reshape(1, C, RX, RY, ZT)


def solution(mesh):
    in_specs = (P(None, None, "gx", "gy", None), P(None, None, None, ("gx", "gy")), P(), P())
    out_specs = P(None, None, "gx", "gy", None)
    return jax.shard_map(shards, mesh=mesh, in_specs=in_specs, out_specs=out_specs, check_vma=False)
```

profile of v0, /device:TPU:25, one launch (start us, length us, event | category | flops | bytes accessed | tf_op | source)
XLA Modules:
  0.0 118.0 jit_solution(17003777431327504790)
XLA Ops:
  0.0 0.0 copy-start.3
  0.0 4.0 %depth_forward.1 = f32[3840,128]{1,0:T(8,128)S(1)} custom-call(f32[20,8,8,768]{3,2,1,0:T(8,128)} %bitcast.9), custom_call_target="tpu_custom_call" | custom-call | flops 1200000000 | bytes 6000000 | tf_op jit(solution)/shard_map/depth_forward/pallas_call | solution.py:211
  4.1 0.0 copy-start
  4.1 30.7 %all_to_all.20 = f32[16,240,128]{2,1,0:T(8,128)S(1)} all-to-all(f32[16,240,128]{2,1,0:T(8,128)S(1)} %bitcast.8), channel_id=1, replica_groups=mesh['gx'=16,'gy'=16] {'gx'}, dimensions={0} | all-to-all | bytes 3932160 | tf_op jit(solution)/shard_map/all_to_all | solution.py:429
  34.8 0.0 copy-start.4
  34.8 0.0 copy-start.5
  34.8 0.0 copy-done.3
  34.8 1.0 x_forward.1
  35.9 23.9 %all_to_all.21.cells = f32[16,8,768]{2,1,0:T(8,128)S(1)} all-to-all(f32[16,8,768]{2,1,0:T(8,128)S(1)} %x_forward.1), channel_id=1, replica_groups={{0,4,8,12,1,5,9,13,2,6,10,14,3,7,11,15},{16,20,24,28,17,21,25,29,18,22,..., dimensions={0} | all-to-all | bytes 786432 | tf_op jit(solution)/shard_map/all_to_all | solution.py:429
  59.8 0.0 copy-done
  59.8 0.0 copy-done.4
  59.8 0.0 copy-done.5
  59.8 0.0 copy-start.2
  59.8 1.7 %y_mix.1 = f32[16,8,768]{2,1,0:T(8,128)S(1)} custom-call(f32[16,8,768]{2,1,0:T(8,128)S(1)} %all_to_all.21.cells, f32[20,20,24,36]{3,2,1,0:T(8,128)S(1)} %copy-done, bf16[48,384]{1,0:T(8,128)(2,1)S(1)} %copy-done.5, bf16[128,144]{1,0:T(8,128)(2,1)S(1)} %copy-done.4), custom_call_target="tpu_custom_call" | custom-call | flops 60000000 | bytes 6000000 | tf_op jit(solution)/shard_map/y_mix/pallas_call | solution.py:303
  61.5 18.4 %all_to_all.22.modes = f32[16,8,768]{2,1,0:T(8,128)S(1)} all-to-all(f32[16,8,768]{2,1,0:T(8,128)S(1)} %y_mix.1), channel_id=1, replica_groups={{0,4,8,12,1,5,9,13,2,6,10,14,3,7,11,15},{16,20,24,28,17,21,25,29,18,22,..., dimensions={0} | all-to-all | bytes 786432 | tf_op jit(solution)/shard_map/all_to_all | solution.py:429
  79.9 0.0 copy-done.2
  79.9 0.0 copy-start.6
  79.9 0.0 copy-start.8
  79.9 1.3 %x_back.1 = f32[3840,128]{1,0:T(8,128)S(1)} custom-call(f32[16,8,768]{2,1,0:T(8,128)S(1)} %all_to_all.22.modes, bf16[2,256,144]{2,1,0:T(8,128)(2,1)S(1)} %copy-done.2), custom_call_target="tpu_custom_call" | custom-call | flops 150000000 | bytes 2500000 | tf_op jit(solution)/shard_map/x_back/pallas_call | solution.py:346
  81.2 0.0 copy-start.1
  81.3 0.0 copy-start.7
  81.3 31.1 %all_to_all.23 = f32[16,240,128]{2,1,0:T(8,128)S(1)} all-to-all(f32[16,240,128]{2,1,0:T(8,128)S(1)} %bitcast.7), channel_id=1, replica_groups=mesh['gx'=16,'gy'=16] {'gx'}, dimensions={0} | all-to-all | bytes 3932160 | tf_op jit(solution)/shard_map/all_to_all | solution.py:429
  112.3 0.0 copy-done.6
  112.3 0.0 copy-done.8
  112.3 0.0 copy-done.1
  112.3 0.0 copy-done.7
  112.3 5.7 %depth_back.1 = f32[20,8,8,768]{3,2,1,0:T(8,128)} custom-call(f32[20,8,8,768]{3,2,1,0:T(8,128)S(1)} %bitcast.10, f32[3840,128]{1,0:T(8,128)S(1)} %bitcast.11, bf16[1152,768]{1,0:T(8,128)(2,1)S(1)} %copy-done.8, f32[20,20]{1,0:T(8,128)S(1)} %copy-done.6, f32[20]{0:T(128)S(1)} %copy-done.7), custom_call_target="tpu_custom_call" | custom-call | flops 3200000000 | bytes 11000000 | tf_op jit(solution)/shard_map/depth_back/pallas_call | solution.py:413
Async XLA Ops:
  0.0 34.8 %copy-start.3 = (bf16[2,48,768]{2,1,0:T(8,128)(2,1)S(1)}, bf16[2,48,768]{2,1,0:T(8,128)(2,1)}, u32[]{:S(2)}) copy-start(bf16[2,48,768]{2,1,0:T(8,128)(2,1)} %constant.10.clone.table) | copy-start | bytes 442372
  4.1 55.7 %copy-start = (f32[20,20,24,36]{3,2,1,0:T(8,128)S(1)}, f32[20,20,24,36]{3,2,1,0:T(8,128)}, u32[]{:S(2)}) copy-start(f32[20,20,24,36]{3,2,1,0:T(8,128)} %weights.1) | copy-start | bytes 4147204
  34.8 25.0 %copy-start.4 = (bf16[128,144]{1,0:T(8,128)(2,1)S(1)}, bf16[128,144]{1,0:T(8,128)(2,1)}, u32[]{:S(2)}) copy-start(bf16[128,144]{1,0:T(8,128)(2,1)} %constant.12.clone.back) | copy-start | bytes 110596
  34.8 25.0 %copy-start.5 = (bf16[48,384]{1,0:T(8,128)(2,1)S(1)}, bf16[48,384]{1,0:T(8,128)(2,1)}, u32[]{:S(2)}) copy-start(bf16[48,384]{1,0:T(8,128)(2,1)} %constant.11.clone.forward) | copy-start | bytes 110596
  59.8 20.1 %copy-start.2 = (bf16[2,256,144]{2,1,0:T(8,128)(2,1)S(1)}, bf16[2,256,144]{2,1,0:T(8,128)(2,1)}, u32[]{:S(2)}) copy-start(bf16[2,256,144]{2,1,0:T(8,128)(2,1)} %constant.13.clone.table) | copy-start | bytes 442372
  79.9 32.4 %copy-start.6 = (f32[20,20]{1,0:T(8,128)S(1)}, f32[20,20]{1,0:T(8,128)}, u32[]{:S(2)}) copy-start(f32[20,20]{1,0:T(8,128)} %channel_map.1) | copy-start | bytes 4804
  79.9 32.4 %copy-start.8 = (bf16[1152,768]{1,0:T(8,128)(2,1)S(1)}, bf16[1152,768]{1,0:T(8,128)(2,1)}, u32[]{:S(2)}) copy-start(bf16[1152,768]{1,0:T(8,128)(2,1)} %constant.14.clone.table) | copy-start | bytes 5308420
  81.2 31.1 %copy-start.1 = (f32[1,20,8,8,768]{4,3,2,1,0:T(8,128)S(1)}, f32[1,20,8,8,768]{4,3,2,1,0:T(8,128)}, u32[]{:S(2)}) copy-start(f32[1,20,8,8,768]{4,3,2,1,0:T(8,128)} %param.9) | copy-start | bytes 11796484
  81.3 31.1 %copy-start.7 = (f32[20]{0:T(128)S(1)}, f32[20]{0:T(128)}, u32[]{:S(2)}) copy-start(f32[20]{0:T(128)} %bias.1) | copy-start | bytes 244
where the time goes:
time: 120 us; the launch traced here: 118 us
  blocking collectives  104 us (87%)
  Pallas kernels  13.8 us (12%)
    all_to_all x4, blocking collectives, exchange(): lax.all_to_all(value, axis, split_axis=0, concat_axis=0, axis_index_group...  104 us
    pallas_call x1, Pallas kernels, final_stage(): pl.pallas_call(final_kernel, in_specs=[whole, whole, whole, whole, pl.Blo...  5.69 us
    pallas_call x1, Pallas kernels, depth_transform(): pl.pallas_call(depth_kernel, in_specs=[pl.BlockSpec(memory_space=pltpu.HB...  4.05 us

commit v1 on v0

--- a/solution.py
+++ b/solution.py
@@ -280,7 +280,7 @@
         reals[i] = real[:, i * HQ : (i + 1) * HQ]
         imags[i] = imag[:, i * HQ : (i + 1) * HQ]
     even_pairs = even_lanes((KY, HQ))
-    group = 4
+    group = 10
     for first in range(0, C, group):
         one = [jnp.zeros((KY, HQ), jnp.float32)] * group
         two = [jnp.zeros((KY, HQ), jnp.float32)] * group
@@ -396,14 +396,8 @@
             for c in range(C):
                 one = value[c * RY : (c + 1) * RY] + bias[c]
                 held[c, x] = 0.5 * one * (1.0 + lax.erf(one * np.float32(np.sqrt(0.5))))
-                first = C // 2 if x == RX - 1 and c >= C // 2 else 0
-                if c == C - 1 or (x == RX - 1 and c == C // 2 - 1):
-                    part = pl.ds(first, c + 1 - first)
-                    copy = pltpu.make_async_copy(
-                        held.at[part, x], out.at[part, x], left.at[len(copies)]
-                    )
-                    copies.append(copy)
-                    copy.start()
+            copies.append(pltpu.make_async_copy(held.at[:, x], out.at[:, x], left.at[x]))
+            copies[-1].start()
     for copy in copies:
         copy.wait()
 
@@ -417,7 +411,7 @@
         out_shape=jax.ShapeDtypeStruct((C, RX, RY, ZT), jnp.float32),
         scratch_shapes=[
             pltpu.VMEM((C, RX, RY, ZT), jnp.float32),
-            pltpu.SemaphoreType.DMA((RX + 1,)),
+            pltpu.SemaphoreType.DMA((RX,)),
         ],
         compiler_params=pltpu.CompilerParams(vmem_limit_bytes=40 * MIB),
         cost_estimate=pl.CostEstimate(flops=3200000000, bytes_accessed=11000000, transcendentals=1000000),

time: 120 us -> 120 us (level)
  no operation moved by 1% of the time
where the time goes in v1:
time: 120 us; the launch traced here: 118 us
  blocking collectives  104 us (87%)
  Pallas kernels  13.8 us (12%)
    all_to_all x4, blocking collectives, exchange(): lax.all_to_all(value, axis, split_axis=0, concat_axis=0, axis_index_group...  104 us
    pallas_call x1, Pallas kernels, final_stage(): pl.pallas_call(final_kernel, in_specs=[whole, whole, whole, whole, pl.Blo...  5.69 us
    pallas_call x1, Pallas kernels, depth_transform(): pl.pallas_call(depth_kernel, in_specs=[pl.BlockSpec(memory_space=pltpu.HB...  4.05 us

profile of v1, /device:TPU:25, one launch (start us, length us, event | category | flops | bytes accessed | tf_op | source)
XLA Modules:
  0.0 118.0 jit_solution(14965869639229490080)
XLA Ops:
  0.0 0.0 copy-start.3
  0.0 4.0 %depth_forward.1 = f32[3840,128]{1,0:T(8,128)S(1)} custom-call(f32[20,8,8,768]{3,2,1,0:T(8,128)} %bitcast.9), custom_call_target="tpu_custom_call" | custom-call | flops 1200000000 | bytes 6000000 | tf_op jit(solution)/shard_map/depth_forward/pallas_call | solution.py:211
  4.1 0.0 copy-start
  4.1 30.7 %all_to_all.20 = f32[16,240,128]{2,1,0:T(8,128)S(1)} all-to-all(f32[16,240,128]{2,1,0:T(8,128)S(1)} %bitcast.8), channel_id=1, replica_groups=mesh['gx'=16,'gy'=16] {'gx'}, dimensions={0} | all-to-all | bytes 3932160 | tf_op jit(solution)/shard_map/all_to_all | solution.py:423
  34.8 0.0 copy-start.4
  34.8 0.0 copy-start.5
  34.8 0.0 copy-done.3
  34.8 1.0 x_forward.1
  35.9 23.9 %all_to_all.21.cells = f32[16,8,768]{2,1,0:T(8,128)S(1)} all-to-all(f32[16,8,768]{2,1,0:T(8,128)S(1)} %x_forward.1), channel_id=1, replica_groups={{0,4,8,12,1,5,9,13,2,6,10,14,3,7,11,15},{16,20,24,28,17,21,25,29,18,22,..., dimensions={0} | all-to-all | bytes 786432 | tf_op jit(solution)/shard_map/all_to_all | solution.py:423
  59.8 0.0 copy-done
  59.8 0.0 copy-done.4
  59.8 0.0 copy-done.5
  59.8 0.0 copy-start.2
  59.8 1.7 %y_mix.1 = f32[16,8,768]{2,1,0:T(8,128)S(1)} custom-call(f32[16,8,768]{2,1,0:T(8,128)S(1)} %all_to_all.21.cells, f32[20,20,24,36]{3,2,1,0:T(8,128)S(1)} %copy-done, bf16[48,384]{1,0:T(8,128)(2,1)S(1)} %copy-done.5, bf16[128,144]{1,0:T(8,128)(2,1)S(1)} %copy-done.4), custom_call_target="tpu_custom_call" | custom-call | flops 60000000 | bytes 6000000 | tf_op jit(solution)/shard_map/y_mix/pallas_call | solution.py:303
  61.5 18.4 %all_to_all.22.modes = f32[16,8,768]{2,1,0:T(8,128)S(1)} all-to-all(f32[16,8,768]{2,1,0:T(8,128)S(1)} %y_mix.1), channel_id=1, replica_groups={{0,4,8,12,1,5,9,13,2,6,10,14,3,7,11,15},{16,20,24,28,17,21,25,29,18,22,..., dimensions={0} | all-to-all | bytes 786432 | tf_op jit(solution)/shard_map/all_to_all | solution.py:423
  79.9 0.0 copy-done.2
  79.9 0.0 copy-start.6
  79.9 0.0 copy-start.8
  79.9 1.3 %x_back.1 = f32[3840,128]{1,0:T(8,128)S(1)} custom-call(f32[16,8,768]{2,1,0:T(8,128)S(1)} %all_to_all.22.modes, bf16[2,256,144]{2,1,0:T(8,128)(2,1)S(1)} %copy-done.2), custom_call_target="tpu_custom_call" | custom-call | flops 150000000 | bytes 2500000 | tf_op jit(solution)/shard_map/x_back/pallas_call | solution.py:346
  81.2 0.0 copy-start.1
  81.2 0.0 copy-start.7
  81.2 31.1 %all_to_all.23 = f32[16,240,128]{2,1,0:T(8,128)S(1)} all-to-all(f32[16,240,128]{2,1,0:T(8,128)S(1)} %bitcast.7), channel_id=1, replica_groups=mesh['gx'=16,'gy'=16] {'gx'}, dimensions={0} | all-to-all | bytes 3932160 | tf_op jit(solution)/shard_map/all_to_all | solution.py:423
  112.3 0.0 copy-done.6
  112.3 0.0 copy-done.8
  112.3 0.0 copy-done.1
  112.3 0.0 copy-done.7
  112.3 5.7 %depth_back.1 = f32[20,8,8,768]{3,2,1,0:T(8,128)} custom-call(f32[20,8,8,768]{3,2,1,0:T(8,128)S(1)} %bitcast.10, f32[3840,128]{1,0:T(8,128)S(1)} %bitcast.11, bf16[1152,768]{1,0:T(8,128)(2,1)S(1)} %copy-done.8, f32[20,20]{1,0:T(8,128)S(1)} %copy-done.6, f32[20]{0:T(128)S(1)} %copy-done.7), custom_call_target="tpu_custom_call" | custom-call | flops 3200000000 | bytes 11000000 | tf_op jit(solution)/shard_map/depth_back/pallas_call | solution.py:407
Async XLA Ops:
  0.0 34.8 %copy-start.3 = (bf16[2,48,768]{2,1,0:T(8,128)(2,1)S(1)}, bf16[2,48,768]{2,1,0:T(8,128)(2,1)}, u32[]{:S(2)}) copy-start(bf16[2,48,768]{2,1,0:T(8,128)(2,1)} %constant.10.clone.table) | copy-start | bytes 442372
  4.1 55.7 %copy-start = (f32[20,20,24,36]{3,2,1,0:T(8,128)S(1)}, f32[20,20,24,36]{3,2,1,0:T(8,128)}, u32[]{:S(2)}) copy-start(f32[20,20,24,36]{3,2,1,0:T(8,128)} %weights.1) | copy-start | bytes 4147204
  34.8 25.0 %copy-start.4 = (bf16[128,144]{1,0:T(8,128)(2,1)S(1)}, bf16[128,144]{1,0:T(8,128)(2,1)}, u32[]{:S(2)}) copy-start(bf16[128,144]{1,0:T(8,128)(2,1)} %constant.12.clone.back) | copy-start | bytes 110596
  34.8 25.0 %copy-start.5 = (bf16[48,384]{1,0:T(8,128)(2,1)S(1)}, bf16[48,384]{1,0:T(8,128)(2,1)}, u32[]{:S(2)}) copy-start(bf16[48,384]{1,0:T(8,128)(2,1)} %constant.11.clone.forward) | copy-start | bytes 110596
  59.8 20.1 %copy-start.2 = (bf16[2,256,144]{2,1,0:T(8,128)(2,1)S(1)}, bf16[2,256,144]{2,1,0:T(8,128)(2,1)}, u32[]{:S(2)}) copy-start(bf16[2,256,144]{2,1,0:T(8,128)(2,1)} %constant.13.clone.table) | copy-start | bytes 442372
  79.9 32.4 %copy-start.6 = (f32[20,20]{1,0:T(8,128)S(1)}, f32[20,20]{1,0:T(8,128)}, u32[]{:S(2)}) copy-start(f32[20,20]{1,0:T(8,128)} %channel_map.1) | copy-start | bytes 4804
  79.9 32.4 %copy-start.8 = (bf16[1152,768]{1,0:T(8,128)(2,1)S(1)}, bf16[1152,768]{1,0:T(8,128)(2,1)}, u32[]{:S(2)}) copy-start(bf16[1152,768]{1,0:T(8,128)(2,1)} %constant.14.clone.table) | copy-start | bytes 5308420
  81.2 31.1 %copy-start.1 = (f32[1,20,8,8,768]{4,3,2,1,0:T(8,128)S(1)}, f32[1,20,8,8,768]{4,3,2,1,0:T(8,128)}, u32[]{:S(2)}) copy-start(f32[1,20,8,8,768]{4,3,2,1,0:T(8,128)} %param.9) | copy-start | bytes 11796484
  81.2 31.1 %copy-start.7 = (f32[20]{0:T(128)S(1)}, f32[20]{0:T(128)}, u32[]{:S(2)}) copy-start(f32[20]{0:T(128)} %bias.1) | copy-start | bytes 244
